TPU v7x, 32 devices: a whole 2x2x4 slice. The times are simulated.
32 devices in a mesh: dp: 4 (over x, core), term: 8 (over z, y).
Axes of the slice: x: 2, y: 2, z: 4, core: 2. Of those that a mesh axis runs over, the one named last changes fastest.
Arguments:
- inputs: bfloat16 [1024, 8192], P('dp'), may hold values from -6 to 6
- cotangent: bfloat16 [1024, 8192], P('dp', 'term'), may hold values from -6 to 6
- logits: float32 [1024, 256], P('dp'), may hold values from -20 to 320
- in_factor: bfloat16 [8192, 2048], P(None, 'term'), may hold values from -0.09375 to 0.09375
- out_factor: bfloat16 [8192, 2048], P(None, 'term'), may hold values from -0.0625 to 0.0625
- expert_factor: bfloat16 [256, 2048], P(None, 'term'), may hold values from -3 to 3
Outputs:
- grad_inputs: bfloat16 [1024, 8192], P('dp', 'term')
- grad_logits: float32 [1024, 256], P('dp', 'term')
- grad_in_factor: float32 [8192, 2048], P('dp', 'term')
- grad_out_factor: float32 [8192, 2048], P('dp', 'term')
- grad_expert_factor: float32 [256, 2048], P('dp', 'term')
All inputs are finite; a program needn't handle non-finite values.
Results may differ from a plain program's by a relative error of at most 0.028.
Values may be sent and summed in bfloat16 or wider, within the bound.
A program may use at most 128 MiB of HBM per device.

v0:
```python
import math
import jax
import jax.numpy as jnp
from jax import lax
from jax.sharding import PartitionSpec as P


def per_device(inputs, cotangent, logits, in_factor, out_factor, expert_factor):
    fl = jnp.float32
    n_term = lax.axis_size("term")
    n_data = lax.axis_size("dp")
    gates = jax.nn.softmax(logits, axis=-1)
    gates_bf = gates.astype(jnp.bfloat16)
    proj_in = jnp.dot(inputs, in_factor, preferred_element_type=fl)
    proj_exp = jnp.dot(gates_bf, expert_factor, preferred_element_type=fl)
    hidden = (proj_in * proj_exp).astype(jnp.bfloat16)
    full_cotan = lax.all_gather(cotangent, "term", axis=1, tiled=True)
    grad_hid = jnp.dot(full_cotan, out_factor, preferred_element_type=fl)
    grad_pin = (grad_hid * proj_exp).astype(jnp.bfloat16)
    grad_pexp = (grad_hid * proj_in).astype(jnp.bfloat16)
    row_total = lax.psum(jnp.sum(grad_hid * proj_in * proj_exp, axis=1, keepdims=True), "term")
    contract_last = (((1,), (1,)), ((), ()))
    part_x = lax.dot_general(grad_pin, in_factor, contract_last, preferred_element_type=fl)
    part_g = lax.dot_general(grad_pexp, expert_factor, contract_last, preferred_element_type=fl)
    sum_x, grad_gate = (
        lax.psum_scatter(
            part_x.astype(jnp.bfloat16), "term", scatter_dimension=1, tiled=True
        ).astype(jnp.float32),
        lax.psum_scatter(
            part_g.astype(jnp.bfloat16), "term", scatter_dimension=1, tiled=True
        ).astype(jnp.float32),
    )
    grad_inputs = sum_x.astype(jnp.bfloat16)
    exp_local = logits.shape[1] // n_term
    gates_local = lax.dynamic_slice_in_dim(gates, lax.axis_index("term") * exp_local, exp_local, 1)
    grad_logits = gates_local * (grad_gate - row_total)
    scale = 1.0 / math.sqrt(inputs.shape[0] * n_data)
    contract_first = (((0,), (0,)), ((), ()))
    part_in = lax.dot_general(inputs, grad_pin, contract_first, preferred_element_type=fl) * scale
    part_out = (
        lax.dot_general(full_cotan, hidden, contract_first, preferred_element_type=fl) * scale
    )
    part_exp = (
        lax.dot_general(gates_bf, grad_pexp, contract_first, preferred_element_type=fl) * scale
    )
    grad_in, grad_out, grad_exp = (
        lax.psum_scatter(
            part_in.astype(jnp.bfloat16), "dp", scatter_dimension=0, tiled=True
        ).astype(jnp.float32),
        lax.psum_scatter(
            part_out.astype(jnp.bfloat16), "dp", scatter_dimension=0, tiled=True
        ).astype(jnp.float32),
        lax.psum_scatter(
            part_exp.astype(jnp.bfloat16), "dp", scatter_dimension=0, tiled=True
        ).astype(jnp.float32),
    )
    return (grad_inputs, grad_logits, grad_in, grad_out, grad_exp)


def solution(mesh):
    return jax.shard_map(
        per_device,
        mesh=mesh,
        in_specs=(
            P("dp", None),
            P("dp", "term"),
            P("dp", None),
            P(None, "term"),
            P(None, "term"),
            P(None, "term"),
        ),
        out_specs=(
            P("dp", "term"),
            P("dp", "term"),
            P("dp", "term"),
            P("dp", "term"),
            P("dp", "term"),
        ),
        check_vma=False,
    )
```

profile of v0, /device:TPU:0, one launch (start us, length us, event | category | flops | bytes accessed | tf_op | source)
XLA Modules:
  0.0 368.6 jit_solution(12951424411813804137)
XLA Ops:
  7.2 0.0 copy-start
  7.2 0.0 all-gather.2.cloned.1.call-start
  7.2 0.7 all-gather.2.cloned.1.call-update
  7.9 0.0 reduce-scatter.14.cloned.1.call-start
  8.0 1.1 copy.11
  9.1 1.1 reduce_max.9
  10.1 0.1 fusion.6
  10.2 5.2 %fusion.11 = f32[256,256]{0,1:T(8,128)S(1)} fusion(bf16[256,8192]{1,0:T(8,128)(2,1)} %param.6, bf16[8192,256]{1,0:T(8,128)(2,1)} %param.9), kind=kOutput, calls=%fused_computation.22 | convolution fusion | flops 1073741824 | bytes 8650752 | tf_op jit(solution)/shard_map/dot_general | solution.py:14
  15.5 70.9 %all-gather.2.cloned.1.call-done = bf16[256,8192]{1,0:T(8,128)(2,1)} async-done(((bf16[256,1024]{1,0:T(8,128)(2,1)}), bf16[256,8192]{1,0:T(8,128)(2,1)}) %all-gather.2.cloned.1.call-update) | async-done | bytes 4194320 | tf_op jit(solution)/shard_map/all_gather | solution.py:17
  86.3 5.2 %fusion.10 = f32[256,256]{0,1:T(8,128)S(1)} fusion(bf16[256,8192]{1,0:T(8,128)(2,1)} %all-gather.2.cloned.1.call-done, bf16[8192,256]{1,0:T(8,128)(2,1)} %param.10), kind=kOutput, calls=%fused_computation.21 | convolution fusion | flops 1073741824 | bytes 8650752 | tf_op jit(solution)/shard_map/dot_general | solution.py:18
  91.5 0.0 copy-done
  91.5 0.3 multiply_reduce_fusion
  91.8 0.9 fusion.4
  92.7 0.0 reduce-scatter.14.cloned.1.call-update
  92.7 0.0 reduce-scatter.8.cloned.1.call-start
  92.7 0.8 convolution_convert_fusion.1
  93.6 0.0 reduce-scatter.8.cloned.1.call-update
  93.6 0.0 reduce-scatter.12.cloned.1.call-start
  93.7 5.4 %fusion.2 = bf16[8192,256]{0,1:T(8,128)(2,1)} fusion(bf16[256,8192]{1,0:T(8,128)(2,1)} %all-gather.2.cloned.1.call-done, f32[256,256]{0,1:T(8,128)S(1)} %fusion.11, f32[256,256]{0,1:T(8,128)S(1)} %get-tuple-element.13), kind=kOutput, calls=%fused_computation.5 | convolution fusion | flops 1078067200 | bytes 8912896 | tf_op jit(solution)/shard_map/dot_general | solution.py:41
  99.1 0.0 reduce-scatter.12.cloned.1.call-update
  99.1 0.0 reduce-scatter.10.cloned.1.call-start
  99.1 5.4 %fusion.3 = bf16[8192,256]{0,1:T(8,128)(2,1)} fusion(bf16[256,256]{0,1:T(8,128)(2,1)S(1)} %get-tuple-element.12, bf16[256,8192]{1,0:T(8,128)(2,1)} %param.6), kind=kOutput, calls=%fused_computation.6 | convolution fusion | flops 1077936128 | bytes 8519680 | tf_op jit(solution)/shard_map/dot_general | solution.py:39
  104.6 0.0 reduce-scatter.10.cloned.1.call-update
  104.6 0.0 reduce-scatter.6.cloned.1.call-start
  104.6 5.5 %convolution_convert_fusion = bf16[256,8192]{1,0:T(8,128)(2,1)} fusion(bf16[256,256]{0,1:T(8,128)(2,1)S(1)} %get-tuple-element.12, bf16[8192,256]{1,0:T(8,128)(2,1)} %param.9), kind=kOutput, calls=%fused_computation.2 | convolution fusion | flops 1075838976 | bytes 8519680 | tf_op jit(solution)/shard_map/dot_general | solution.py:23
  110.1 0.0 reduce-scatter.6.cloned.1.call-update
  110.2 18.7 %psum.7 = f32[256]{0:T(256)S(1)} all-reduce(f32[256]{0:T(256)S(1)} %get-tuple-element.10), channel_id=1, replica_groups=mesh['dp'=4,'term'=8] {'term'}, use_global_device_ids=true, to_apply=%region_5.0 | all-reduce | flops 256 | bytes 2048 | tf_op jit(solution)/shard_map/psum | solution.py:21
  128.9 0.0 reduce-scatter.14.cloned.1.call-done
  128.9 1.4 convert_element_type.61
  130.3 45.6 %reduce-scatter.8.cloned.1.call-done = bf16[256,32]{0,1:T(8,128)(2,1)} async-done(((bf16[256,256]{0,1:T(8,128)(2,1)}), bf16[256,32]{0,1:T(8,128)(2,1)}) %reduce-scatter.8.cloned.1.call-update) | async-done | bytes 16400 | tf_op jit(solution)/shard_map/reduce_scatter | solution.py:29
  175.9 1.3 subtract_multiply_fusion
  177.2 44.8 %reduce-scatter.12.cloned.1.call-done = bf16[2048,256]{0,1:T(8,128)(2,1)} async-done(((bf16[8192,256]{0,1:T(8,128)(2,1)}), bf16[2048,256]{0,1:T(8,128)(2,1)}) %reduce-scatter.12.cloned.1.call-update) | async-done | bytes 1048592 | tf_op jit(solution)/shard_map/reduce_scatter | solution.py:50
  222.0 2.6 copy.13
  224.6 44.4 %reduce-scatter.10.cloned.1.call-done = bf16[2048,256]{0,1:T(8,128)(2,1)} async-done(((bf16[8192,256]{0,1:T(8,128)(2,1)}), bf16[2048,256]{0,1:T(8,128)(2,1)}) %reduce-scatter.10.cloned.1.call-update) | async-done | bytes 1048592 | tf_op jit(solution)/shard_map/reduce_scatter | solution.py:47
  268.9 2.6 copy.12
  271.5 90.3 %reduce-scatter.6.cloned.1.call-done = bf16[256,1024]{1,0:T(8,128)(2,1)} async-done(((bf16[256,8192]{1,0:T(8,128)(2,1)}), bf16[256,1024]{1,0:T(8,128)(2,1)}) %reduce-scatter.6.cloned.1.call-update) | async-done | bytes 524304 | tf_op jit(solution)/shard_map/reduce_scatter | solution.py:26
  (1 shorter events, 0.0 us)
Async XLA Ops:
  7.2 84.4 %copy-start = (bf16[256,256]{1,0:T(8,128)(2,1)S(1)}, bf16[256,256]{1,0:T(8,128)(2,1)}, u32[]{:S(2)}) copy-start(bf16[256,256]{1,0:T(8,128)(2,1)} %param.11) | copy-start | bytes 393220
  7.2 79.1 %all-gather.2.cloned.1.call-start = ((), (), s32[]{:S(2)}) async-start(), calls=%async_computation.5 | async-start | bytes 4718592 | tf_op jit(solution)/shard_map/all_gather | solution.py:17
  7.9 121.0 %reduce-scatter.14.cloned.1.call-start = ((), (), s32[]{:S(2)}) async-start(), calls=%async_computation.10 | async-start | bytes 163840 | tf_op jit(solution)/shard_map/reduce_scatter | solution.py:53
  92.7 83.2 %reduce-scatter.8.cloned.1.call-start = ((), (), s32[]{:S(2)}) async-start(), calls=%async_computation.7 | async-start | bytes 147456 | tf_op jit(solution)/shard_map/reduce_scatter | solution.py:29
  93.6 128.4 %reduce-scatter.12.cloned.1.call-start = ((), (), s32[]{:S(2)}) async-start(), calls=%async_computation.9 | async-start | bytes 5242880 | tf_op jit(solution)/shard_map/reduce_scatter | solution.py:50
  99.1 169.8 %reduce-scatter.10.cloned.1.call-start = ((), (), s32[]{:S(2)}) async-start(), calls=%async_computation.8 | async-start | bytes 5242880 | tf_op jit(solution)/shard_map/reduce_scatter | solution.py:47
  104.6 257.2 %reduce-scatter.6.cloned.1.call-start = ((), (), s32[]{:S(2)}) async-start(), calls=%async_computation.6 | async-start | bytes 4718592 | tf_op jit(solution)/shard_map/reduce_scatter | solution.py:26
Sparse Core Ops, SparseCore 0:
  10.2 76.0 all-gather.1
  92.8 17.8 reduce-scatter.13
  114.9 60.8 reduce-scatter.7
  178.4 43.5 reduce-scatter.11
  224.4 44.4 reduce-scatter.9
  273.4 88.2 reduce-scatter.5
where the time goes:
time: 369 us
  waiting for transfers between devices  297 us (80%)
  matrix products  28.7 us (8%)
  blocking collectives  18.7 us (5%)
  between operations  14.2 us (4%)
  local copies, waits for them, and re-layouts  6.21 us (2%)
  other arithmetic  3.91 us (1%)
    reduce_scatter x1, waiting for transfers between devices, per_device(): lax.psum_scatter(part_x.astype(jnp.bfloat16), 'term', scatter_dimension=1...  90.3 us
    all_gather x1, waiting for transfers between devices, per_device(): full_cotan = lax.all_gather(cotangent, 'term', axis=1, tiled=True)  70.9 us
    reduce_scatter x1, waiting for transfers between devices, per_device(): lax.psum_scatter(part_g.astype(jnp.bfloat16), 'term', scatter_dimension=1...  45.6 us
    reduce_scatter x1, waiting for transfers between devices, per_device(): lax.psum_scatter(part_out.astype(jnp.bfloat16), 'dp', scatter_dimension=0...  44.8 us
    reduce_scatter x1, waiting for transfers between devices, per_device(): lax.psum_scatter(part_in.astype(jnp.bfloat16), 'dp', scatter_dimension=0,...  44.4 us
    psum x1, blocking collectives, per_device(): lax.psum(jnp.sum(grad_hid * proj_in * proj_exp, axis=1, keepdims=True), '...  18.7 us
  transfers between devices with their start and end apart: 6, of which 5 were waited for; matrix products, arithmetic and copies ran while one was open for 9% of the time, Pallas kernels for 0%

commit v1 on v0

--- a/solution.py
+++ b/solution.py
@@ -18,7 +18,10 @@
     grad_hid = jnp.dot(full_cotan, out_factor, preferred_element_type=fl)
     grad_pin = (grad_hid * proj_exp).astype(jnp.bfloat16)
     grad_pexp = (grad_hid * proj_in).astype(jnp.bfloat16)
-    row_total = lax.psum(jnp.sum(grad_hid * proj_in * proj_exp, axis=1, keepdims=True), "term")
+    row_total = jnp.sum(
+        lax.all_gather(jnp.sum(grad_hid * proj_in * proj_exp, axis=1, keepdims=True), "term"),
+        axis=0,
+    )
     contract_last = (((1,), (1,)), ((), ()))
     part_x = lax.dot_general(grad_pin, in_factor, contract_last, preferred_element_type=fl)
     part_g = lax.dot_general(grad_pexp, expert_factor, contract_last, preferred_element_type=fl)

time: 369 us -> 369 us (level)
    psum x1 -> x0, blocking collectives: 18.7 us -> none  [per_device(): lax.psum(jnp.sum(grad_hid * proj_in * proj_exp, axis=1, keepdims=True), '...]
    all_gather x0 -> x1, blocking collectives: none -> 17.9 us  [per_device(): lax.all_gather(jnp.sum(grad_hid * proj_in * proj_exp, axis=1, keepdims=Tr...]
where the time goes in v1:
time: 369 us
  waiting for transfers between devices  297 us (80%)
  matrix products  28.7 us (8%)
  blocking collectives  17.9 us (5%)
  between operations  14.2 us (4%)
  local copies, waits for them, and re-layouts  6.21 us (2%)
  other arithmetic  3.94 us (1%)
    reduce_scatter x1, waiting for transfers between devices, per_device(): lax.psum_scatter(part_x.astype(jnp.bfloat16), 'term', scatter_dimension=1...  90.3 us
    all_gather x1, waiting for transfers between devices, per_device(): full_cotan = lax.all_gather(cotangent, 'term', axis=1, tiled=True)  70.9 us
    reduce_scatter x1, waiting for transfers between devices, per_device(): lax.psum_scatter(part_g.astype(jnp.bfloat16), 'term', scatter_dimension=1...  46.4 us
    reduce_scatter x1, waiting for transfers between devices, per_device(): lax.psum_scatter(part_out.astype(jnp.bfloat16), 'dp', scatter_dimension=0...  44.8 us
    reduce_scatter x1, waiting for transfers between devices, per_device(): lax.psum_scatter(part_in.astype(jnp.bfloat16), 'dp', scatter_dimension=0,...  44.4 us
    all_gather x1, blocking collectives, per_device(): lax.all_gather(jnp.sum(grad_hid * proj_in * proj_exp, axis=1, keepdims=Tr...  17.9 us
  transfers between devices with their start and end apart: 6, of which 5 were waited for; matrix products, arithmetic and copies ran while one was open for 9% of the time, Pallas kernels for 0%

profile of v1, /device:TPU:0, one launch (start us, length us, event | category | flops | bytes accessed | tf_op | source)
XLA Modules:
  0.0 368.6 jit_solution(2575955475367786367)
XLA Ops:
  7.2 0.0 copy-start
  7.2 0.0 all-gather.4.cloned.1.call-start
  7.2 0.7 all-gather.4.cloned.1.call-update
  7.9 0.0 reduce-scatter.14.cloned.1.call-start
  8.0 1.1 copy.14
  9.1 1.1 reduce_max.9
  10.1 0.1 fusion.6
  10.2 5.2 %fusion.11 = f32[256,256]{0,1:T(8,128)S(1)} fusion(bf16[256,8192]{1,0:T(8,128)(2,1)} %param.6, bf16[8192,256]{1,0:T(8,128)(2,1)} %param.9), kind=kOutput, calls=%fused_computation.22 | convolution fusion | flops 1073741824 | bytes 8650752 | tf_op jit(solution)/shard_map/dot_general | solution.py:14
  15.5 70.9 %all-gather.4.cloned.1.call-done = bf16[256,8192]{1,0:T(8,128)(2,1)} async-done(((bf16[256,1024]{1,0:T(8,128)(2,1)}), bf16[256,8192]{1,0:T(8,128)(2,1)}) %all-gather.4.cloned.1.call-update) | async-done | bytes 4194320 | tf_op jit(solution)/shard_map/all_gather | solution.py:17
  86.3 5.2 %fusion.10 = f32[256,256]{0,1:T(8,128)S(1)} fusion(bf16[256,8192]{1,0:T(8,128)(2,1)} %all-gather.4.cloned.1.call-done, bf16[8192,256]{1,0:T(8,128)(2,1)} %param.10), kind=kOutput, calls=%fused_computation.21 | convolution fusion | flops 1073741824 | bytes 8650752 | tf_op jit(solution)/shard_map/dot_general | solution.py:18
  91.5 0.0 copy-done
  91.5 0.3 multiply_reduce_fusion
  91.8 0.9 fusion.4
  92.7 0.0 reduce-scatter.14.cloned.1.call-update
  92.7 0.0 reduce-scatter.8.cloned.1.call-start
  92.7 0.8 convolution_convert_fusion.1
  93.6 0.0 reduce-scatter.8.cloned.1.call-update
  93.6 0.0 reduce-scatter.12.cloned.1.call-start
  93.7 5.4 %fusion.2 = bf16[8192,256]{0,1:T(8,128)(2,1)} fusion(bf16[256,8192]{1,0:T(8,128)(2,1)} %all-gather.4.cloned.1.call-done, f32[256,256]{0,1:T(8,128)S(1)} %fusion.11, f32[256,256]{0,1:T(8,128)S(1)} %get-tuple-element.18), kind=kOutput, calls=%fused_computation.5 | convolution fusion | flops 1078067200 | bytes 8912896 | tf_op jit(solution)/shard_map/dot_general | solution.py:44
  99.1 0.0 reduce-scatter.12.cloned.1.call-update
  99.1 0.0 reduce-scatter.10.cloned.1.call-start
  99.1 5.4 %fusion.3 = bf16[8192,256]{0,1:T(8,128)(2,1)} fusion(bf16[256,256]{0,1:T(8,128)(2,1)S(1)} %get-tuple-element.17, bf16[256,8192]{1,0:T(8,128)(2,1)} %param.6), kind=kOutput, calls=%fused_computation.6 | convolution fusion | flops 1077936128 | bytes 8519680 | tf_op jit(solution)/shard_map/dot_general | solution.py:42
  104.6 0.0 reduce-scatter.10.cloned.1.call-update
  104.6 0.0 reduce-scatter.6.cloned.1.call-start
  104.6 5.5 %convolution_convert_fusion = bf16[256,8192]{1,0:T(8,128)(2,1)} fusion(bf16[256,256]{0,1:T(8,128)(2,1)S(1)} %get-tuple-element.17, bf16[8192,256]{1,0:T(8,128)(2,1)} %param.9), kind=kOutput, calls=%fused_computation.2 | convolution fusion | flops 1075838976 | bytes 8519680 | tf_op jit(solution)/shard_map/dot_general | solution.py:26
  110.1 0.0 reduce-scatter.6.cloned.1.call-update
  110.2 17.9 %all-gather.1 = f32[8,1,256]{2,1,0:T(1,128)S(1)} all-gather(f32[1,1,256]{2,1,0:T(1,128)S(1)} %bitcast.18), channel_id=2, replica_groups=mesh['dp'=4,'term'=8] {'term'}, dimensions={0}, use_global_device_ids=true | all-gather | bytes 9216 | tf_op jit(solution)/shard_map/all_gather | solution.py:22
  128.0 0.0 reduce-scatter.14.cloned.1.call-done
  128.1 1.4 convert_element_type.61
  129.5 46.4 %reduce-scatter.8.cloned.1.call-done = bf16[256,32]{0,1:T(8,128)(2,1)} async-done(((bf16[256,256]{0,1:T(8,128)(2,1)}), bf16[256,32]{0,1:T(8,128)(2,1)}) %reduce-scatter.8.cloned.1.call-update) | async-done | bytes 16400 | tf_op jit(solution)/shard_map/reduce_scatter | solution.py:32
  175.9 1.3 subtract_multiply_fusion
  177.2 44.8 %reduce-scatter.12.cloned.1.call-done = bf16[2048,256]{0,1:T(8,128)(2,1)} async-done(((bf16[8192,256]{0,1:T(8,128)(2,1)}), bf16[2048,256]{0,1:T(8,128)(2,1)}) %reduce-scatter.12.cloned.1.call-update) | async-done | bytes 1048592 | tf_op jit(solution)/shard_map/reduce_scatter | solution.py:53
  222.0 2.6 copy.16
  224.6 44.4 %reduce-scatter.10.cloned.1.call-done = bf16[2048,256]{0,1:T(8,128)(2,1)} async-done(((bf16[8192,256]{0,1:T(8,128)(2,1)}), bf16[2048,256]{0,1:T(8,128)(2,1)}) %reduce-scatter.10.cloned.1.call-update) | async-done | bytes 1048592 | tf_op jit(solution)/shard_map/reduce_scatter | solution.py:50
  268.9 2.6 copy.15
  271.5 90.3 %reduce-scatter.6.cloned.1.call-done = bf16[256,1024]{1,0:T(8,128)(2,1)} async-done(((bf16[256,8192]{1,0:T(8,128)(2,1)}), bf16[256,1024]{1,0:T(8,128)(2,1)}) %reduce-scatter.6.cloned.1.call-update) | async-done | bytes 524304 | tf_op jit(solution)/shard_map/reduce_scatter | solution.py:29
  (2 shorter events, 0.1 us)
Async XLA Ops:
  7.2 84.4 %copy-start = (bf16[256,256]{1,0:T(8,128)(2,1)S(1)}, bf16[256,256]{1,0:T(8,128)(2,1)}, u32[]{:S(2)}) copy-start(bf16[256,256]{1,0:T(8,128)(2,1)} %param.11) | copy-start | bytes 393220
  7.2 79.1 %all-gather.4.cloned.1.call-start = ((), (), s32[]{:S(2)}) async-start(), calls=%async_computation.5 | async-start | bytes 4718592 | tf_op jit(solution)/shard_map/all_gather | solution.py:17
  7.9 120.1 %reduce-scatter.14.cloned.1.call-start = ((), (), s32[]{:S(2)}) async-start(), calls=%async_computation.10 | async-start | bytes 163840 | tf_op jit(solution)/shard_map/reduce_scatter | solution.py:56
  92.7 83.2 %reduce-scatter.8.cloned.1.call-start = ((), (), s32[]{:S(2)}) async-start(), calls=%async_computation.7 | async-start | bytes 147456 | tf_op jit(solution)/shard_map/reduce_scatter | solution.py:32
  93.6 128.4 %reduce-scatter.12.cloned.1.call-start = ((), (), s32[]{:S(2)}) async-start(), calls=%async_computation.9 | async-start | bytes 5242880 | tf_op jit(solution)/shard_map/reduce_scatter | solution.py:53
  99.1 169.8 %reduce-scatter.10.cloned.1.call-start = ((), (), s32[]{:S(2)}) async-start(), calls=%async_computation.8 | async-start | bytes 5242880 | tf_op jit(solution)/shard_map/reduce_scatter | solution.py:50
  104.6 257.2 %reduce-scatter.6.cloned.1.call-start = ((), (), s32[]{:S(2)}) async-start(), calls=%async_computation.6 | async-start | bytes 4718592 | tf_op jit(solution)/shard_map/reduce_scatter | solution.py:29
Sparse Core Ops, SparseCore 0:
  10.2 76.0 all-gather.3
  92.8 17.8 reduce-scatter.13
  114.9 60.8 reduce-scatter.7
  178.4 43.5 reduce-scatter.11
  224.4 44.4 reduce-scatter.9
  273.4 88.2 reduce-scatter.5
